TPU v7x, 128 devices: a whole 4x4x4 slice. The times are simulated.
128 devices in a mesh: ctx: 16 (over y, x), head: 8 (over z, core).
Axes of the slice: x: 4, y: 4, z: 4, core: 2. Of those that a mesh axis runs over, the one named last changes fastest.
Arguments:
- query_input: bfloat16 [16, 1024, 4096], P('ctx', 'head'), may hold values from -6 to 6
- key_input: bfloat16 [16, 1024, 512], P('ctx', 'head'), may hold values from -6 to 6
- value_input: bfloat16 [16, 1024, 512], P('ctx', 'head'), may hold values from -6 to 6
- grad_input: bfloat16 [16, 1024, 4096], P('ctx', 'head'), may hold values from -6 to 6
Outputs:
- attended: bfloat16 [16, 1024, 4096], P('ctx', 'head')
- query_grad: float32 [16, 1024, 4096], P('ctx', 'head')
- key_grad: float32 [16, 1024, 512], P('ctx', 'head')
- value_grad: float32 [16, 1024, 512], P('ctx', 'head')
All inputs are finite; a program needn't handle non-finite values.
Results may differ from a plain program's by a relative error of at most 0.0076.
Values may be sent and summed in bfloat16 or wider, within the bound.
No kernel may reach another device: no remote copies, remote signals or barrier semaphores. Data moves between devices by JAX's collectives and lax.ppermute only.
A program may use at most 192 MiB of HBM per device.

v0:
```python
import math
import jax
import jax.numpy as jnp
from jax import lax
from jax.sharding import PartitionSpec as P

HD = 128


def from_partner(value, axis, apart):
    mask = 2**apart
    pairs = [(source, source ^ mask) for source in range(lax.axis_size(axis))]
    return lax.ppermute(value, axis, pairs)


def sent_together(arrays, axis, dim, along):
    both = jnp.concatenate(arrays, axis=along)
    filled, at, outs = (lax.all_gather(both, axis, axis=dim, tiled=True), 0, [])
    for a in arrays:
        outs.append(lax.slice_in_dim(filled, at, at + a.shape[along], axis=along))
        at += a.shape[along]
    return tuple(outs)


def attend(query_split, grad_split, query_pos, key_all, value_all, key_span, scaling):
    rows, pair_heads, sharing, head_dim = query_split.shape
    block_total = (jnp.max(query_pos) + key_span) // key_span

    def block_scores(begin_row):
        key_block = lax.dynamic_slice_in_dim(key_all, begin_row, key_span, 0).reshape(
            key_span, pair_heads, head_dim
        )
        raw_scores = (
            jnp.einsum("ihgd,jhd->hgij", query_split, key_block, preferred_element_type=jnp.float32)
            * scaling
        )
        allowed = (begin_row + jnp.arange(key_span, dtype=jnp.int32))[None, :] <= query_pos[:, None]
        return (jnp.where(allowed, raw_scores, -jnp.inf), key_block)

    def value_slice(begin_row):
        return lax.dynamic_slice_in_dim(value_all, begin_row, key_span, 0).reshape(
            key_span, pair_heads, head_dim
        )

    def stats_pass(step_num, state_in):
        running_max, running_sum = state_in
        scores, unused = block_scores(step_num * key_span)
        highest = jnp.maximum(running_max, jnp.max(scores, axis=-1))
        rescale = jnp.exp(running_max - highest)
        running_sum = running_sum * rescale + jnp.sum(jnp.exp(scores - highest[..., None]), axis=-1)
        return (highest, running_sum)

    stat_shape = (pair_heads, sharing, rows)
    highest, running_sum = lax.fori_loop(
        0,
        block_total,
        stats_pass,
        (jnp.full(stat_shape, -jnp.inf, jnp.float32), jnp.zeros(stat_shape, jnp.float32)),
    )
    log_total = highest + jnp.log(running_sum)

    def output_pass(step_num, running_out):
        begin_row = step_num * key_span
        scores, unused = block_scores(begin_row)
        weights = jnp.exp(scores - log_total[..., None]).astype(jnp.bfloat16)
        return running_out + jnp.einsum(
            "hgij,jhd->hgid", weights, value_slice(begin_row), preferred_element_type=jnp.float32
        )

    running_out = lax.fori_loop(
        0, block_total, output_pass, jnp.zeros(stat_shape + (head_dim,), jnp.float32)
    )
    attended = running_out.transpose(2, 0, 1, 3).astype(jnp.bfloat16)
    row_dot = jnp.sum(
        grad_split.astype(jnp.float32) * attended.astype(jnp.float32), axis=-1
    ).transpose(1, 2, 0)

    def grad_pass(step_num, state_in):
        begin_row = step_num * key_span
        scores, key_block = block_scores(begin_row)
        value_block = value_slice(begin_row)
        normalized = jnp.exp(scores - log_total[..., None])
        weights = normalized.astype(jnp.bfloat16)
        weight_grad = jnp.einsum(
            "ihgd,jhd->hgij", grad_split, value_block, preferred_element_type=jnp.float32
        )
        score_grad = (normalized * (weight_grad - row_dot[..., None])).astype(jnp.bfloat16)
        query_sum = state_in[0] + jnp.einsum(
            "hgij,jhd->ihgd", score_grad, key_block, preferred_element_type=jnp.float32
        )
        return (query_sum,)

    query_zero = jnp.zeros((rows, pair_heads, sharing, head_dim), jnp.float32)
    initial = (query_zero,)
    gradients = lax.fori_loop(0, block_total, grad_pass, initial)
    sums_out = None
    return (attended, gradients[0], sums_out, log_total, row_dot)


def on_device(query_input, key_input, value_input, grad_input):
    local_rows = query_input.shape[1]
    query_width = query_input.shape[2]
    pair_width = key_input.shape[2]
    pair_heads = pair_width // HD
    sharing = query_width // pair_width
    local_heads = pair_heads * sharing
    block_count = lax.axis_size("ctx")
    block_rows = 2 * local_rows
    all_rows = block_count * block_rows
    key_span = min(512, all_rows)
    scaling = 1.0 / math.sqrt(HD)
    block_index = lax.axis_index("ctx")
    half_index = lax.axis_index("head") % 2
    block_first = block_index * block_rows
    first_row = block_first + half_index * local_rows
    query_local = query_input.reshape(local_rows, query_width)
    grad_local = grad_input.reshape(local_rows, query_width)
    own_pairs = jnp.stack(
        [key_input.reshape(local_rows, pair_width), value_input.reshape(local_rows, pair_width)]
    )
    partner_pairs = from_partner(own_pairs, "head", 0)
    block_pairs = jnp.where(
        half_index == 0,
        jnp.concatenate([own_pairs, partner_pairs], axis=1),
        jnp.concatenate([partner_pairs, own_pairs], axis=1),
    )
    gathered_pairs = lax.all_gather(block_pairs, "ctx", axis=1, tiled=True)
    key_all = gathered_pairs[0]
    value_all = gathered_pairs[1]
    query_split = query_local.reshape(local_rows, pair_heads, sharing, HD)
    grad_split = grad_local.reshape(local_rows, pair_heads, sharing, HD)
    query_pos = first_row + jnp.arange(local_rows, dtype=jnp.int32)
    sums_in = None
    attended, query_sum, sums_out, log_total, row_dot = attend(
        query_split, grad_split, query_pos, key_all, value_all, key_span, scaling
    )
    query_grad = scaling * query_sum
    total_rows = log_total.reshape(local_heads, local_rows).T
    dot_rows = row_dot.reshape(local_heads, local_rows).T
    total_all, dot_all = sent_together((total_rows, dot_rows), "ctx", 0, 1)
    block_keys = block_pairs[0].reshape(block_rows, pair_heads, HD)
    block_values = block_pairs[1].reshape(block_rows, pair_heads, HD)
    key_pos = block_first + jnp.arange(block_rows, dtype=jnp.int32)
    zero_rows = jnp.zeros((block_rows, pair_width), jnp.float32)
    query_piece, grad_piece = sent_together((query_local, grad_local), "ctx", 0, 1)
    piece_rows = query_piece.shape[0]
    query_span = math.gcd(piece_rows, 512)
    span_total = piece_rows // query_span

    def one_block(step_num, sums_in):
        offset = step_num * query_span
        gathered_index = offset + jnp.arange(query_span, dtype=jnp.int32)
        row_pos = (
            gathered_index // local_rows * block_rows
            + half_index * local_rows
            + gathered_index % local_rows
        )

        def accumulate(sums_now):
            query_block = lax.dynamic_slice_in_dim(query_piece, offset, query_span, 0).reshape(
                query_span, pair_heads, sharing, HD
            )
            grad_block = lax.dynamic_slice_in_dim(grad_piece, offset, query_span, 0).reshape(
                query_span, pair_heads, sharing, HD
            )
            total_block = lax.dynamic_slice_in_dim(total_all, offset, query_span, 0).T.reshape(
                pair_heads, sharing, query_span
            )
            dot_block = lax.dynamic_slice_in_dim(dot_all, offset, query_span, 0).T.reshape(
                pair_heads, sharing, query_span
            )
            raw_scores = (
                jnp.einsum(
                    "ihgd,jhd->hgij", query_block, block_keys, preferred_element_type=jnp.float32
                )
                * scaling
            )
            allowed = key_pos[None, :] <= row_pos[:, None]
            normalized = jnp.exp(jnp.where(allowed, raw_scores, -jnp.inf) - total_block[..., None])
            weights = normalized.astype(jnp.bfloat16)
            weight_grad = jnp.einsum(
                "ihgd,jhd->hgij", grad_block, block_values, preferred_element_type=jnp.float32
            )
            score_grad = (normalized * (weight_grad - dot_block[..., None])).astype(jnp.bfloat16)
            key_add = jnp.einsum(
                "hgij,ihgd->jhd", score_grad, query_block, preferred_element_type=jnp.float32
            ).reshape(block_rows, pair_width)
            value_add = jnp.einsum(
                "hgij,ihgd->jhd", weights, grad_block, preferred_element_type=jnp.float32
            ).reshape(block_rows, pair_width)
            return (sums_now[0] + key_add, sums_now[1] + value_add)

        def unchanged(sums_now):
            return sums_now

        return lax.cond(jnp.max(row_pos) >= block_first, accumulate, unchanged, sums_in)

    key_sum, value_sum = lax.fori_loop(0, span_total, one_block, (zero_rows, zero_rows))
    outgoing = jnp.stack(
        [
            lax.dynamic_slice_in_dim(key_sum, (1 - half_index) * local_rows, local_rows, 0),
            lax.dynamic_slice_in_dim(value_sum, (1 - half_index) * local_rows, local_rows, 0),
        ]
    )
    incoming = from_partner(outgoing.astype(jnp.bfloat16), "head", 0).astype(outgoing.dtype)
    key_mine = (
        lax.dynamic_slice_in_dim(key_sum, half_index * local_rows, local_rows, 0) + incoming[0]
    )
    value_mine = (
        lax.dynamic_slice_in_dim(value_sum, half_index * local_rows, local_rows, 0) + incoming[1]
    )
    key_grad = scaling * key_mine
    return (
        attended.reshape(1, local_rows, query_width),
        query_grad.reshape(1, local_rows, query_width),
        key_grad.reshape(1, local_rows, pair_width),
        value_mine.reshape(1, local_rows, pair_width),
    )


def solution(mesh):
    in_specs = (
        P("ctx", "head", None),
        P("ctx", "head", None),
        P("ctx", "head", None),
        P("ctx", "head", None),
    )
    out_specs = (
        P("ctx", "head", None),
        P("ctx", "head", None),
        P("ctx", "head", None),
        P("ctx", "head", None),
    )
    return jax.shard_map(
        on_device, mesh=mesh, in_specs=in_specs, out_specs=out_specs, check_vma=False
    )
```

profile of v0, /device:TPU:1, one launch (start us, length us, event | category | flops | bytes accessed | tf_op | source)
XLA Modules:
  0.0 464.3 jit_solution(15359233953880189449)
XLA Ops:
  9.0 1.5 collective-permute-start
  12.8 1.6 copy.69
  14.4 1.6 copy.76
  23.0 62.7 %all-gather.3.cloned.1.call-done = bf16[2,4096,512]{2,1,0:T(8,128)(2,1)} async-done(((bf16[2,256,512]{2,1,0:T(8,128)(2,1)}), bf16[2,4096,512]{2,1,0:T(8,128)(2,1)}) %all-gather.3.cloned.1.call-update) | async-done | bytes 8388624 | tf_op jit(solution)/shard_map/all_gather | solution.py:127
  85.7 5.7 %slice_bitcast_fusion = (bf16[4096,512]{1,0:T(8,128)(2,1)}, bf16[4096,512]{1,0:T(8,128)(2,1)}) fusion(bf16[2,4096,512]{2,1,0:T(8,128)(2,1)} %all-gather.3.cloned.1.call-done), kind=kLoop, calls=%fused_computation.84 | loop fusion | bytes 16777216 | tf_op jit(solution)/shard_map/squeeze | solution.py:129
  91.4 6.4 %copy.72 = bf16[4096,512]{0,1:T(8,128)(2,1)} copy(bf16[4096,512]{1,0:T(8,128)(2,1)} %get-tuple-element.831) | data formatting | bytes 8388608
  97.8 6.7 %copy.74 = bf16[4096,512]{0,1:T(8,128)(2,1)} copy(bf16[4096,512]{1,0:T(8,128)(2,1)} %get-tuple-element.830) | data formatting | bytes 8388608
  104.5 4.6 while.54
  107.2 1.8 exponential_reduce_fusion.2
  109.1 1.6 broadcast_in_dim.55
  110.7 7.7 %while.55 = (s32[]{:T(128)}, f32[4,8,128,128]{3,2,1,0:T(8,128)}, s32[]{:T(128)}, bf16[4096,512]{0,1:T(8,128)(2,1)}, bf16[128,4,8,128]{3,0,2,1:T(8,128)(2,1)S(1)}...) while((s32[]{:T(128)}, f32[4,8,128,128]{3,2,1,0:T(8,128)}, ...), condition=%wide.region_6.7_spmd.clone, body=%wide.region_5.6_spmd.clone.sunk | while | flops 1082720896 | bytes 8541367 | solution.py:70
  112.1 6.2 %fusion.108 = f32[4,8,128,128]{3,2,1,0:T(8,128)} fusion(f32[4,8,128,128]{3,2,1,0:T(8,128)} %get-tuple-element.1133, bf16[512,4,128,1]{0,2,3,1:T(8,128)(2,1)S(1)} %bitcast.231, f32[4,8,128]{2,1,0:T(8,128)S(1)} %get-tuple-element.1149, pred[128,512]{0,1:T(8,128)(4,1)S(1)} %broadcast_compare_fusion.8, bf16[512,4,128,1]{0,2,3,1:T(8,128)(2,1)S(1)} %bitcast.232, ...), kind=kOutput, calls=%fused_computation.46.clone.1 | convolution fusion | flops 1082654720 | bytes 6373376 | tf_op jit(solution)/shard_map/while/body/hgij,jhd->hgid/dot_general | solution.py:66
  118.4 1.9 copy.75
  122.2 109.7 %all_gather.11 = f32[2048,64]{0,1:T(8,128)S(1)} all-gather(f32[128,64]{0,1:T(8,128)S(1)} %pad_maximum_fusion.2), channel_id=1, replica_groups=mesh['ctx'=16,'head'=8] {'ctx'}, dimensions={0}, use_global_device_ids=true | all-gather | bytes 557056 | tf_op jit(solution)/shard_map/all_gather | solution.py:18
  232.7 1.6 broadcast_in_dim.58
  234.3 14.4 %while.56 = (s32[]{:T(128)}, f32[128,4,8,128]{0,3,2,1:T(8,128)}, s32[]{:T(128)}, bf16[4096,512]{0,1:T(8,128)(2,1)}, bf16[128,4,8,128]{3,0,2,1:T(8,128)(2,1)S(1)}...) while((s32[]{:T(128)}, f32[128,4,8,128]{0,3,2,1:T(8,128)}, ...), condition=%wide.region_9.10_spmd.clone, body=%wide.region_8.9_spmd.clone.sunk | while | flops 1623786112 | bytes 31102180 | solution.py:95
  235.7 4.5 fusion.115
  240.3 8.3 %bitcast_add_fusion.4 = f32[128,4,8,128]{0,3,2,1:T(8,128)} fusion(f32[128,4,8,128]{0,3,2,1:T(8,128)} %get-tuple-element.1171, bf16[512,4,128,1]{0,2,3,1:T(8,128)(2,1)S(1)} %bitcast.225, f32[4,512,128,8]{2,1,3,0:T(8,128)} %fusion.115, f32[4,8,128]{2,1,0:T(8,128)S(1)} %get-tuple-element.1192, f32[4,8,128]{2,1,0:T(8,128)S(1)} %get-tuple-element.1189, ...), kind=kOutput, calls=%fused_computation.63.clone.1 | convolution fusion | flops 1086849024 | bytes 14778368 | tf_op jit(solution)/shard_map/while/body/hgij,jhd->ihgd/dot_general | solution.py:88
  248.7 48.5 %all-gather.5.cloned.1.call-done = bf16[2048,8192]{0,1:T(8,128)(2,1)} async-done(((bf16[128,8192]{0,1:T(8,128)(2,1)}), bf16[2048,8192]{0,1:T(8,128)(2,1)}) %all-gather.5.cloned.1.call-update) | async-done | bytes 33554448 | tf_op jit(solution)/shard_map/all_gather | solution.py:18
  297.2 23.5 %fusion.67 = (bf16[2048,4096]{0,1:T(8,128)(2,1)}, bf16[2048,4096]{0,1:T(8,128)(2,1)}) fusion(bf16[2048,8192]{0,1:T(8,128)(2,1)} %all-gather.5.cloned.1.call-done), kind=kLoop, calls=%fused_computation.107 | loop fusion | bytes 67108864 | tf_op jit(solution)/shard_map/slice | solution.py:20
  320.7 129.3 %while.57 = (s32[]{:T(128)}, f32[256,512]{0,1:T(8,128)S(1)}, f32[256,512]{0,1:T(8,128)S(1)}, s32[]{:T(128)}, s32[]{:T(128)}, /*index=5*/bf16[2048,4096]{0,1:T(8,...) while((s32[]{:T(128)}, f32[256,512]{0,1:T(8,128)S(1)}, ...), condition=%wide.region_14.15_spmd.clone.clone, body=%wide.region_10.14_spmd.clone.clone.sunk | while | flops 4337315840 | bytes 174399952 | solution.py:198
  322.0 31.0 %conditional.4 = ((f32[256,512]{0,1:T(8,128)S(1)}, f32[256,512]{0,1:T(8,128)S(1)})) conditional(s32[]{:T(128)} %convert_element_type.67, (f32[256,512]{0,1:T(8,128)S(1)}, f32[256,512]{0,1:T(8,128)S(1)}) %tuple.142, (s32[]{:T(128)}, bf16[2048,4096]{0,1:T(8,128)(2,1)}, s32[]{:T(128)}, s32[512]{0:T(512)S(1)}, bf16[256,4,128]{2,0,1:T(8,128)(2,1)S(1)}, ...), branch_computations={%region_12.12_spmd, %region_13.13_spmd} | conditional | flops 4337303552 | bytes 174396576 | solution.py:196
  322.1 4.4 constant_dynamic-slice_fusion
  326.5 2.5 constant_dynamic-slice_fusion.1
  329.0 2.4 fusion.18
  332.4 7.7 %fusion.12 = f32[4,128,256,1]{2,1,3,0:T(8,128)S(1)} fusion(bf16[512,4,8,128]{0,3,2,1:T(8,128)(2,1)} %bitcast.222, f32[4,512,8,256]{3,1,2,0:T(8,128)S(1)} %fusion.18, f32[4,8,512]{2,1,0:T(8,128)S(1)} %dynamic-slice_bitcast_fusion.1, pred[512,256]{1,0:T(8,128)(4,1)S(1)} %broadcast_compare_fusion), kind=kOutput, calls=%fused_computation.10 | convolution fusion | flops 1090519040 | bytes 21692416 | tf_op jit(solution)/shard_map/while/body/eval_jaxpr/cond/branch_1_fun/hgij,ihgd->jhd/dot_general | solution.py:188
  341.0 11.8 %fusion.15 = f32[4,128,256,1]{2,1,3,0:T(8,128)S(1)} fusion(bf16[512,4,8,128]{0,3,2,1:T(8,128)(2,1)} %bitcast.221, f32[4,512,8,256]{3,1,2,0:T(8,128)} %copy-done, bf16[512,4,8,128]{0,3,2,1:T(8,128)(2,1)} %bitcast.223, f32[4,8,512]{2,1,0:T(8,128)S(1)} %dynamic-slice_bitcast_fusion, f32[4,8,512]{2,1,0:T(8,128)S(1)} %dynamic-slice_bitcast_fusion.1, ...), kind=kOutput, calls=%fused_computation.12 | convolution fusion | flops 2172649472 | bytes 26214400 | tf_op jit(solution)/shard_map/while/body/eval_jaxpr/cond/branch_1_fun/hgij,ihgd->jhd/dot_general | solution.py:185
  354.4 31.0 %conditional.4 = ((f32[256,512]{0,1:T(8,128)S(1)}, f32[256,512]{0,1:T(8,128)S(1)})) conditional(s32[]{:T(128)} %convert_element_type.67, (f32[256,512]{0,1:T(8,128)S(1)}, f32[256,512]{0,1:T(8,128)S(1)}) %tuple.142, (s32[]{:T(128)}, bf16[2048,4096]{0,1:T(8,128)(2,1)}, s32[]{:T(128)}, s32[512]{0:T(512)S(1)}, bf16[256,4,128]{2,0,1:T(8,128)(2,1)S(1)}, ...), branch_computations={%region_12.12_spmd, %region_13.13_spmd} | conditional | flops 4337303552 | bytes 174396576 | solution.py:196
  354.4 4.4 constant_dynamic-slice_fusion
  358.8 2.5 constant_dynamic-slice_fusion.1
  361.3 2.4 fusion.18
  364.8 7.7 %fusion.12 = f32[4,128,256,1]{2,1,3,0:T(8,128)S(1)} fusion(bf16[512,4,8,128]{0,3,2,1:T(8,128)(2,1)} %bitcast.222, f32[4,512,8,256]{3,1,2,0:T(8,128)S(1)} %fusion.18, f32[4,8,512]{2,1,0:T(8,128)S(1)} %dynamic-slice_bitcast_fusion.1, pred[512,256]{1,0:T(8,128)(4,1)S(1)} %broadcast_compare_fusion), kind=kOutput, calls=%fused_computation.10 | convolution fusion | flops 1090519040 | bytes 21692416 | tf_op jit(solution)/shard_map/while/body/eval_jaxpr/cond/branch_1_fun/hgij,ihgd->jhd/dot_general | solution.py:188
  373.4 11.8 %fusion.15 = f32[4,128,256,1]{2,1,3,0:T(8,128)S(1)} fusion(bf16[512,4,8,128]{0,3,2,1:T(8,128)(2,1)} %bitcast.221, f32[4,512,8,256]{3,1,2,0:T(8,128)} %copy-done, bf16[512,4,8,128]{0,3,2,1:T(8,128)(2,1)} %bitcast.223, f32[4,8,512]{2,1,0:T(8,128)S(1)} %dynamic-slice_bitcast_fusion, f32[4,8,512]{2,1,0:T(8,128)S(1)} %dynamic-slice_bitcast_fusion.1, ...), kind=kOutput, calls=%fused_computation.12 | convolution fusion | flops 2172649472 | bytes 26214400 | tf_op jit(solution)/shard_map/while/body/eval_jaxpr/cond/branch_1_fun/hgij,ihgd->jhd/dot_general | solution.py:185
  386.7 31.0 %conditional.4 = ((f32[256,512]{0,1:T(8,128)S(1)}, f32[256,512]{0,1:T(8,128)S(1)})) conditional(s32[]{:T(128)} %convert_element_type.67, (f32[256,512]{0,1:T(8,128)S(1)}, f32[256,512]{0,1:T(8,128)S(1)}) %tuple.142, (s32[]{:T(128)}, bf16[2048,4096]{0,1:T(8,128)(2,1)}, s32[]{:T(128)}, s32[512]{0:T(512)S(1)}, bf16[256,4,128]{2,0,1:T(8,128)(2,1)S(1)}, ...), branch_computations={%region_12.12_spmd, %region_13.13_spmd} | conditional | flops 4337303552 | bytes 174396576 | solution.py:196
  386.7 4.4 constant_dynamic-slice_fusion
  391.1 2.5 constant_dynamic-slice_fusion.1
  393.6 2.4 fusion.18
  397.1 7.7 %fusion.12 = f32[4,128,256,1]{2,1,3,0:T(8,128)S(1)} fusion(bf16[512,4,8,128]{0,3,2,1:T(8,128)(2,1)} %bitcast.222, f32[4,512,8,256]{3,1,2,0:T(8,128)S(1)} %fusion.18, f32[4,8,512]{2,1,0:T(8,128)S(1)} %dynamic-slice_bitcast_fusion.1, pred[512,256]{1,0:T(8,128)(4,1)S(1)} %broadcast_compare_fusion), kind=kOutput, calls=%fused_computation.10 | convolution fusion | flops 1090519040 | bytes 21692416 | tf_op jit(solution)/shard_map/while/body/eval_jaxpr/cond/branch_1_fun/hgij,ihgd->jhd/dot_general | solution.py:188
  405.7 11.8 %fusion.15 = f32[4,128,256,1]{2,1,3,0:T(8,128)S(1)} fusion(bf16[512,4,8,128]{0,3,2,1:T(8,128)(2,1)} %bitcast.221, f32[4,512,8,256]{3,1,2,0:T(8,128)} %copy-done, bf16[512,4,8,128]{0,3,2,1:T(8,128)(2,1)} %bitcast.223, f32[4,8,512]{2,1,0:T(8,128)S(1)} %dynamic-slice_bitcast_fusion, f32[4,8,512]{2,1,0:T(8,128)S(1)} %dynamic-slice_bitcast_fusion.1, ...), kind=kOutput, calls=%fused_computation.12 | convolution fusion | flops 2172649472 | bytes 26214400 | tf_op jit(solution)/shard_map/while/body/eval_jaxpr/cond/branch_1_fun/hgij,ihgd->jhd/dot_general | solution.py:185
  419.0 31.0 %conditional.4 = ((f32[256,512]{0,1:T(8,128)S(1)}, f32[256,512]{0,1:T(8,128)S(1)})) conditional(s32[]{:T(128)} %convert_element_type.67, (f32[256,512]{0,1:T(8,128)S(1)}, f32[256,512]{0,1:T(8,128)S(1)}) %tuple.142, (s32[]{:T(128)}, bf16[2048,4096]{0,1:T(8,128)(2,1)}, s32[]{:T(128)}, s32[512]{0:T(512)S(1)}, bf16[256,4,128]{2,0,1:T(8,128)(2,1)S(1)}, ...), branch_computations={%region_12.12_spmd, %region_13.13_spmd} | conditional | flops 4337303552 | bytes 174396576 | solution.py:196
  419.0 4.4 constant_dynamic-slice_fusion
  423.4 2.5 constant_dynamic-slice_fusion.1
  425.9 2.4 fusion.18
  429.4 7.7 %fusion.12 = f32[4,128,256,1]{2,1,3,0:T(8,128)S(1)} fusion(bf16[512,4,8,128]{0,3,2,1:T(8,128)(2,1)} %bitcast.222, f32[4,512,8,256]{3,1,2,0:T(8,128)S(1)} %fusion.18, f32[4,8,512]{2,1,0:T(8,128)S(1)} %dynamic-slice_bitcast_fusion.1, pred[512,256]{1,0:T(8,128)(4,1)S(1)} %broadcast_compare_fusion), kind=kOutput, calls=%fused_computation.10 | convolution fusion | flops 1090519040 | bytes 21692416 | tf_op jit(solution)/shard_map/while/body/eval_jaxpr/cond/branch_1_fun/hgij,ihgd->jhd/dot_general | solution.py:188
  438.0 11.8 %fusion.15 = f32[4,128,256,1]{2,1,3,0:T(8,128)S(1)} fusion(bf16[512,4,8,128]{0,3,2,1:T(8,128)(2,1)} %bitcast.221, f32[4,512,8,256]{3,1,2,0:T(8,128)} %copy-done, bf16[512,4,8,128]{0,3,2,1:T(8,128)(2,1)} %bitcast.223, f32[4,8,512]{2,1,0:T(8,128)S(1)} %dynamic-slice_bitcast_fusion, f32[4,8,512]{2,1,0:T(8,128)S(1)} %dynamic-slice_bitcast_fusion.1, ...), kind=kOutput, calls=%fused_computation.12 | convolution fusion | flops 2172649472 | bytes 26214400 | tf_op jit(solution)/shard_map/while/body/eval_jaxpr/cond/branch_1_fun/hgij,ihgd->jhd/dot_general | solution.py:185
  451.3 1.6 collective-permute-start.1
  452.9 1.8 broadcast_multiply_fusion
  454.7 1.8 copy.109
  (109 shorter events, 32.1 us)
Async XLA Ops:
  7.2 78.5 %all-gather.3.cloned.1.call-start = ((), (), s32[]{:S(2)}) async-start(), calls=%async_computation | async-start | bytes 8912896 | tf_op jit(solution)/shard_map/all_gather | solution.py:127
  9.0 2.7 collective-permute-start
  12.7 284.4 %all-gather.5.cloned.1.call-start = ((), (), s32[]{:S(2)}) async-start(), calls=%async_computation.1 | async-start | bytes 35651584 | tf_op jit(solution)/shard_map/all_gather | solution.py:18
  234.3 6.0 %copy-start.4 = (bf16[128,4,8,128]{3,0,2,1:T(8,128)(2,1)S(1)}, bf16[128,4,8,128]{3,0,2,1:T(8,128)(2,1)}, u32[]{:S(2)}) copy-start(bf16[128,4,8,128]{3,0,2,1:T(8,128)(2,1)} %get-tuple-element.1191) | copy-start | bytes 3145732 | tf_op jit(solution)/shard_map/while
  328.9 2.4 copy-start.1
  331.4 8.8 %copy-start = (f32[4,512,8,256]{3,1,2,0:T(8,128)}, f32[4,512,8,256]{3,1,2,0:T(8,128)S(1)}, u32[]{:S(2)}) copy-start(f32[4,512,8,256]{3,1,2,0:T(8,128)S(1)} %fusion.18) | copy-start | bytes 50331652 | tf_op jit(solution)/shard_map/while/body/eval_jaxpr/cond
  332.4 8.6 %copy-start.5 = (bf16[256,4,128]{2,0,1:T(8,128)(2,1)S(1)}, bf16[256,4,128]{2,0,1:T(8,128)(2,1)}, u32[]{:S(2)}) copy-start(bf16[256,4,128]{2,0,1:T(8,128)(2,1)} %get-tuple-element.452) | copy-start | bytes 786436 | tf_op jit(solution)/shard_map/while/body/eval_jaxpr/cond
  361.3 2.4 copy-start.1
  363.7 8.8 %copy-start = (f32[4,512,8,256]{3,1,2,0:T(8,128)}, f32[4,512,8,256]{3,1,2,0:T(8,128)S(1)}, u32[]{:S(2)}) copy-start(f32[4,512,8,256]{3,1,2,0:T(8,128)S(1)} %fusion.18) | copy-start | bytes 50331652 | tf_op jit(solution)/shard_map/while/body/eval_jaxpr/cond
  364.8 8.6 %copy-start.5 = (bf16[256,4,128]{2,0,1:T(8,128)(2,1)S(1)}, bf16[256,4,128]{2,0,1:T(8,128)(2,1)}, u32[]{:S(2)}) copy-start(bf16[256,4,128]{2,0,1:T(8,128)(2,1)} %get-tuple-element.452) | copy-start | bytes 786436 | tf_op jit(solution)/shard_map/while/body/eval_jaxpr/cond
  393.6 2.4 copy-start.1
  396.0 8.8 %copy-start = (f32[4,512,8,256]{3,1,2,0:T(8,128)}, f32[4,512,8,256]{3,1,2,0:T(8,128)S(1)}, u32[]{:S(2)}) copy-start(f32[4,512,8,256]{3,1,2,0:T(8,128)S(1)} %fusion.18) | copy-start | bytes 50331652 | tf_op jit(solution)/shard_map/while/body/eval_jaxpr/cond
  397.1 8.6 %copy-start.5 = (bf16[256,4,128]{2,0,1:T(8,128)(2,1)S(1)}, bf16[256,4,128]{2,0,1:T(8,128)(2,1)}, u32[]{:S(2)}) copy-start(bf16[256,4,128]{2,0,1:T(8,128)(2,1)} %get-tuple-element.452) | copy-start | bytes 786436 | tf_op jit(solution)/shard_map/while/body/eval_jaxpr/cond
  425.9 2.4 copy-start.1
  428.3 8.8 %copy-start = (f32[4,512,8,256]{3,1,2,0:T(8,128)}, f32[4,512,8,256]{3,1,2,0:T(8,128)S(1)}, u32[]{:S(2)}) copy-start(f32[4,512,8,256]{3,1,2,0:T(8,128)S(1)} %fusion.18) | copy-start | bytes 50331652 | tf_op jit(solution)/shard_map/while/body/eval_jaxpr/cond
  429.4 8.6 %copy-start.5 = (bf16[256,4,128]{2,0,1:T(8,128)(2,1)S(1)}, bf16[256,4,128]{2,0,1:T(8,128)(2,1)}, u32[]{:S(2)}) copy-start(bf16[256,4,128]{2,0,1:T(8,128)(2,1)} %get-tuple-element.452) | copy-start | bytes 786436 | tf_op jit(solution)/shard_map/while/body/eval_jaxpr/cond
  450.4 2.4 copy-start.2
  451.3 5.2 %collective-permute-start.1 = (bf16[2,128,512]{2,1,0:T(8,128)(2,1)}, bf16[2,128,512]{2,1,0:T(8,128)(2,1)S(1)}, u32[]{:S(2)}, u32[]{:S(2)}) collective-permute-start(bf16[2,128,512]{2,1,0:T(8,128)(2,1)} %pad_maximum_fusion.1), channel_id=1, source_target_pairs={{0,1},{1,0},{2,3},{3,2},{4,5},{5,4},{6,7},{7,6},{8,9},{9,8},{10,11... | collective-permute-start | bytes 786440 | tf_op jit(solution)/shard_map/ppermute | solution.py:13
  452.9 3.7 copy-start.3
Sparse Core Ops, SparseCore 0:
  12.9 72.7 all-gather.2
  87.8 209.3 all-gather.4
where the time goes:
time: 466 us; the launch traced here: 464 us
  waiting for transfers between devices  112 us (24%)
  blocking collectives  110 us (24%)
  matrix products  108 us (23%)
  local copies, waits for them, and re-layouts  99.7 us (21%)
  between operations  14.9 us (3%)
  other arithmetic  13.3 us (3%)
    all_gather x1, blocking collectives, sent_together(): filled, at, outs = (lax.all_gather(both, axis, axis=dim, tiled=True), 0, [])  110 us
    all_gather x1, waiting for transfers between devices, on_device(): gathered_pairs = lax.all_gather(block_pairs, 'ctx', axis=1, tiled=True)  62.7 us
    all_gather x1, waiting for transfers between devices, sent_together(): filled, at, outs = (lax.all_gather(both, axis, axis=dim, tiled=True), 0, [])  48.5 us
    dot_general x4, matrix products, accumulate(): jnp.einsum('hgij,ihgd->jhd', score_grad, query_block, preferred_element_t...  47.2 us
    dot_general x4, matrix products, accumulate(): jnp.einsum('hgij,ihgd->jhd', weights, grad_block, preferred_element_type=...  30.9 us
    slice x2, local copies, waits for them, and re-layouts, sent_together(): outs.append(lax.slice_in_dim(filled, at, at + a.shape[along], axis=along))  24.3 us
    unnamed x16, local copies, waits for them, and re-layouts  21.7 us
    dynamic_slice x4, local copies, waits for them, and re-layouts, accumulate(): lax.dynamic_slice_in_dim(grad_piece, offset, query_span, 0)  17.7 us
  transfers between devices with their start and end apart: 4, of which 3 were waited for; matrix products, arithmetic and copies ran while one was open for 14% of the time, Pallas kernels for 0%

commit v1 on v0

--- a/solution.py
+++ b/solution.py
@@ -5,6 +5,11 @@
 from jax.sharding import PartitionSpec as P
 
 HD = 128
+
+
+def gather_over(x, axis, dim):
+    sent = jnp.stack([x] * lax.axis_size(axis))
+    return jnp.concatenate(lax.all_to_all(sent, axis, 0, 0), axis=dim)
 
 
 def from_partner(value, axis, apart):
@@ -124,7 +129,7 @@
         jnp.concatenate([own_pairs, partner_pairs], axis=1),
         jnp.concatenate([partner_pairs, own_pairs], axis=1),
     )
-    gathered_pairs = lax.all_gather(block_pairs, "ctx", axis=1, tiled=True)
+    gathered_pairs = gather_over(block_pairs, "ctx", 1)
     key_all = gathered_pairs[0]
     value_all = gathered_pairs[1]
     query_split = query_local.reshape(local_rows, pair_heads, sharing, HD)

time: 466 us -> 538 us (1.15)
  the two profiles are of different devices: /device:TPU:1 before, /device:TPU:71 now
where the time goes in v1:
time: 538 us; the launch traced here: 536 us
  matrix products  158 us (29%)
  waiting for transfers between devices  133 us (25%)
  local copies, waits for them, and re-layouts  104 us (19%)
  blocking collectives  96.4 us (18%)
  between operations  14.9 us (3%)
  other arithmetic  14.8 us (3%)
  starting transfers between devices  11.7 us (2%)
    all_to_all x1, waiting for transfers between devices, gather_over(): return jnp.concatenate(lax.all_to_all(sent, axis, 0, 0), axis=dim)  132 us
    all_gather x1, blocking collectives, sent_together(): filled, at, outs = (lax.all_gather(both, axis, axis=dim, tiled=True), 0, [])  96.4 us
    dot_general x4, matrix products, accumulate(): jnp.einsum('hgij,ihgd->jhd', score_grad, query_block, preferred_element_t...  47.1 us
    dot_general x4, matrix products, accumulate(): jnp.einsum('hgij,ihgd->jhd', weights, grad_block, preferred_element_type=...  36.2 us
    dot_general x4, matrix products, accumulate(): jnp.einsum('ihgd,jhd->hgij', query_block, block_keys, preferred_element_t...  32.5 us
    dynamic_slice x4, local copies, waits for them, and re-layouts, accumulate(): lax.dynamic_slice_in_dim(grad_piece, offset, query_span, 0)  23.7 us
    slice x2, local copies, waits for them, and re-layouts, sent_together(): outs.append(lax.slice_in_dim(filled, at, at + a.shape[along], axis=along))  23.5 us
    unnamed x21, local copies, waits for them, and re-layouts  21 us
  transfers between devices with their start and end apart: 4, of which 2 were waited for; matrix products, arithmetic and copies ran while one was open for 17% of the time, Pallas kernels for 0%

profile of v1, /device:TPU:71, one launch (start us, length us, event | category | flops | bytes accessed | tf_op | source)
XLA Modules:
  0.0 535.8 jit_solution(14777611810489807151)
XLA Ops:
  14.6 4.2 stack.14
  18.8 6.9 %all-to-all-start = ((bf16[16,2,256,512]{3,2,1,0:T(8,128)(2,1)}), bf16[16,2,256,512]{3,2,1,0:T(8,128)(2,1)}, u32[]{:S(2)}, u32[]{:S(2)}) async-start(bf16[16,2,256,512]{3,2,1,0:T(8,128)(2,1)} %stack.14), calls=%async_computation | async-start | bytes 16777216 | tf_op jit(solution)/shard_map/all_to_all | solution.py:12
  31.1 131.9 %all-to-all-done = bf16[16,2,256,512]{3,2,1,0:T(8,128)(2,1)} async-done(((bf16[16,2,256,512]{3,2,1,0:T(8,128)(2,1)}), bf16[16,2,256,512]{3,2,1,0:T(8,128)(2,1)}, u32[]{:S(2)}, u32[]{:S(2)}) %all-to-all-start) | async-done | bytes 8388640 | tf_op jit(solution)/shard_map/all_to_all | solution.py:12
  163.0 5.9 %fusion.68 = (bf16[1,16,256,512]{3,2,0,1:T(8,128)(2,1)}, bf16[1,16,256,512]{3,2,0,1:T(8,128)(2,1)}) fusion(bf16[2,16,256,512]{3,2,0,1:T(8,128)(2,1)} %bitcast.20), kind=kLoop, calls=%fused_computation.105 | loop fusion | bytes 16777216 | tf_op jit(solution)/shard_map/slice | solution.py:134
  168.8 6.4 %copy.83 = bf16[4096,512]{0,1:T(8,128)(2,1)} copy(bf16[4096,512]{1,0:T(8,128)(2,1)} %bitcast.231) | data formatting | bytes 8388608
  175.2 6.6 %copy.81 = bf16[4096,512]{0,1:T(8,128)(2,1)} copy(bf16[4096,512]{1,0:T(8,128)(2,1)} %bitcast.230) | data formatting | bytes 8388608
  181.8 9.2 %while.54 = (s32[]{:T(128)}, f32[4,8,128]{2,1,0:T(8,128)S(1)}, f32[4,8,128]{2,1,0:T(8,128)S(1)}, s32[]{:T(128)}, bf16[4096,512]{0,1:T(8,128)(2,1)}, /*index=5*/b...) while((s32[]{:T(128)}, f32[4,8,128]{2,1,0:T(8,128)S(1)}, ...), condition=%wide.region_4.5_spmd.clone, body=%wide.region_1.4_spmd.clone.sunk | while | flops 551625344 | bytes 19813544 | solution.py:59
  184.5 1.8 exponential_reduce_fusion.2
  189.1 1.8 exponential_reduce_fusion.2
  192.6 15.4 %while.55 = (s32[]{:T(128)}, f32[4,8,128,128]{3,2,1,0:T(8,128)}, s32[]{:T(128)}, bf16[4096,512]{0,1:T(8,128)(2,1)}, bf16[128,4,8,128]{3,0,2,1:T(8,128)(2,1)S(1)}...) while((s32[]{:T(128)}, f32[4,8,128,128]{3,2,1,0:T(8,128)}, ...), condition=%wide.region_6.7_spmd.clone, body=%wide.region_5.6_spmd.clone.sunk | while | flops 1082720896 | bytes 8541359 | solution.py:75
  194.1 6.3 %fusion.109 = f32[4,8,128,128]{3,2,1,0:T(8,128)} fusion(f32[4,8,128,128]{3,2,1,0:T(8,128)} %get-tuple-element.1123, bf16[512,4,128,1]{0,2,3,1:T(8,128)(2,1)S(1)} %bitcast.233, f32[4,8,128]{2,1,0:T(8,128)S(1)} %get-tuple-element.1139, pred[128,512]{0,1:T(8,128)(4,1)S(1)} %broadcast_compare_fusion.8, bf16[512,4,128,1]{0,2,3,1:T(8,128)(2,1)S(1)} %bitcast.234, ...), kind=kOutput, calls=%fused_computation.46.clone.1 | convolution fusion | flops 1082654720 | bytes 6373376 | tf_op jit(solution)/shard_map/while/body/hgij,jhd->hgid/dot_general | solution.py:71
  201.8 6.2 %fusion.109 = f32[4,8,128,128]{3,2,1,0:T(8,128)} fusion(f32[4,8,128,128]{3,2,1,0:T(8,128)} %get-tuple-element.1123, bf16[512,4,128,1]{0,2,3,1:T(8,128)(2,1)S(1)} %bitcast.233, f32[4,8,128]{2,1,0:T(8,128)S(1)} %get-tuple-element.1139, pred[128,512]{0,1:T(8,128)(4,1)S(1)} %broadcast_compare_fusion.8, bf16[512,4,128,1]{0,2,3,1:T(8,128)(2,1)S(1)} %bitcast.234, ...), kind=kOutput, calls=%fused_computation.46.clone.1 | convolution fusion | flops 1082654720 | bytes 6373376 | tf_op jit(solution)/shard_map/while/body/hgij,jhd->hgid/dot_general | solution.py:71
  208.0 1.8 copy.84
  211.8 96.4 %all_gather.7 = f32[2048,64]{0,1:T(8,128)S(1)} all-gather(f32[128,64]{0,1:T(8,128)S(1)} %pad_maximum_fusion.3), channel_id=1, replica_groups=mesh['ctx'=16,'head'=8] {'ctx'}, dimensions={0}, use_global_device_ids=true | all-gather | bytes 557056 | tf_op jit(solution)/shard_map/all_gather | solution.py:23
  309.8 29.1 %while.56 = (s32[]{:T(128)}, f32[128,4,8,128]{0,3,2,1:T(8,128)}, s32[]{:T(128)}, bf16[4096,512]{0,1:T(8,128)(2,1)}, bf16[128,4,8,128]{3,0,2,1:T(8,128)(2,1)S(1)}...) while((s32[]{:T(128)}, f32[128,4,8,128]{0,3,2,1:T(8,128)}, ...), condition=%wide.region_9.10_spmd.clone, body=%wide.region_8.9_spmd.clone.sunk | while | flops 1623786112 | bytes 26907840 | solution.py:100
  311.2 4.5 fusion.116
  315.7 8.6 %bitcast_add_fusion.4 = f32[128,4,8,128]{0,3,2,1:T(8,128)} fusion(f32[128,4,8,128]{0,3,2,1:T(8,128)} %get-tuple-element.1161, bf16[512,4,128,1]{0,2,3,1:T(8,128)(2,1)S(1)} %bitcast.225, f32[4,512,128,8]{2,1,3,0:T(8,128)} %fusion.116, f32[4,8,128]{2,1,0:T(8,128)S(1)} %get-tuple-element.1182, f32[4,8,128]{2,1,0:T(8,128)S(1)} %get-tuple-element.1179, ...), kind=kOutput, calls=%fused_computation.63.clone.1 | convolution fusion | flops 1086849024 | bytes 14778368 | tf_op jit(solution)/shard_map/while/body/hgij,jhd->ihgd/dot_general | solution.py:93
  325.8 4.5 fusion.116
  330.3 8.6 %bitcast_add_fusion.4 = f32[128,4,8,128]{0,3,2,1:T(8,128)} fusion(f32[128,4,8,128]{0,3,2,1:T(8,128)} %get-tuple-element.1161, bf16[512,4,128,1]{0,2,3,1:T(8,128)(2,1)S(1)} %bitcast.225, f32[4,512,128,8]{2,1,3,0:T(8,128)} %fusion.116, f32[4,8,128]{2,1,0:T(8,128)S(1)} %get-tuple-element.1182, f32[4,8,128]{2,1,0:T(8,128)S(1)} %get-tuple-element.1179, ...), kind=kOutput, calls=%fused_computation.63.clone.1 | convolution fusion | flops 1086849024 | bytes 14778368 | tf_op jit(solution)/shard_map/while/body/hgij,jhd->ihgd/dot_general | solution.py:93
  338.9 23.5 %fusion.67 = (bf16[2048,4096]{0,1:T(8,128)(2,1)}, bf16[2048,4096]{0,1:T(8,128)(2,1)}) fusion(bf16[2048,8192]{0,1:T(8,128)(2,1)} %all-gather.2.cloned.1.call-done), kind=kLoop, calls=%fused_computation.104 | loop fusion | bytes 67108864 | tf_op jit(solution)/shard_map/slice | solution.py:25
  362.5 156.7 %while.57 = (s32[]{:T(128)}, f32[256,512]{0,1:T(8,128)S(1)}, f32[256,512]{0,1:T(8,128)S(1)}, s32[]{:T(128)}, s32[]{:T(128)}, /*index=5*/bf16[2048,4096]{0,1:T(8,...) while((s32[]{:T(128)}, f32[256,512]{0,1:T(8,128)S(1)}, ...), condition=%wide.region_14.15_spmd.clone.clone, body=%wide.region_10.14_spmd.clone.clone.sunk | while | flops 4337315840 | bytes 106242424 | solution.py:203
  363.9 37.8 %conditional.4 = ((f32[256,512]{0,1:T(8,128)S(1)}, f32[256,512]{0,1:T(8,128)S(1)})) conditional(s32[]{:T(128)} %convert_element_type.67, (f32[256,512]{0,1:T(8,128)S(1)}, f32[256,512]{0,1:T(8,128)S(1)}) %tuple.141, (s32[]{:T(128)}, bf16[2048,4096]{0,1:T(8,128)(2,1)}, s32[]{:T(128)}, s32[512]{0:T(512)S(1)}, bf16[256,4,128]{2,0,1:T(8,128)(2,1)S(1)}, ...), branch_computations={%region_12.12_spmd, %region_13.13_spmd} | conditional | flops 4337303552 | bytes 106239080 | solution.py:201
  364.1 2.5 constant_dynamic-slice_fusion.1
  366.6 5.9 %constant_dynamic-slice_fusion = bf16[512,4096]{0,1:T(8,128)(2,1)} fusion(bf16[2048,4096]{0,1:T(8,128)(2,1)} %get-tuple-element.451, s32[]{:T(128)S(6)} %select_n.83), kind=kLoop, calls=%fused_computation.21 | loop fusion | bytes 8388612 | tf_op jit(solution)/shard_map/while/body/eval_jaxpr/cond/branch_1_fun/dynamic_slice | solution.py:168
  372.5 8.1 %fusion.18 = f32[4,512,8,256]{3,1,2,0:T(8,128)} fusion(bf16[512,4,8,128]{0,3,2,1:T(8,128)(2,1)S(1)} %bitcast.220, bf16[256,4,128]{2,0,1:T(8,128)(2,1)S(1)} %get-tuple-element.449), kind=kOutput, calls=%fused_computation.16 | convolution fusion | flops 1073741824 | bytes 21233664 | tf_op jit(solution)/shard_map/while/body/eval_jaxpr/cond/branch_1_fun/ihgd,jhd->hgij/dot_general | solution.py:178
  380.7 11.8 %fusion.15 = f32[4,128,256,1]{2,1,3,0:T(8,128)S(1)} fusion(bf16[512,4,8,128]{0,3,2,1:T(8,128)(2,1)} %bitcast.221, f32[4,512,8,256]{3,1,2,0:T(8,128)} %fusion.18, bf16[512,4,8,128]{0,3,2,1:T(8,128)(2,1)} %bitcast.222, f32[4,8,512]{2,1,0:T(8,128)S(1)} %dynamic-slice_bitcast_fusion, f32[4,8,512]{2,1,0:T(8,128)S(1)} %dynamic-slice_bitcast_fusion.1, ...), kind=kOutput, calls=%fused_computation.12 | convolution fusion | flops 2172649472 | bytes 26214400 | tf_op jit(solution)/shard_map/while/body/eval_jaxpr/cond/branch_1_fun/hgij,ihgd->jhd/dot_general | solution.py:190
  392.4 9.1 %fusion.12 = f32[4,128,256,1]{2,1,3,0:T(8,128)S(1)} fusion(bf16[512,4,8,128]{0,3,2,1:T(8,128)(2,1)} %bitcast.223, f32[4,512,8,256]{3,1,2,0:T(8,128)} %fusion.18, f32[4,8,512]{2,1,0:T(8,128)S(1)} %dynamic-slice_bitcast_fusion.1, pred[512,256]{1,0:T(8,128)(4,1)S(1)} %broadcast_compare_fusion), kind=kOutput, calls=%fused_computation.10 | convolution fusion | flops 1090519040 | bytes 21692416 | tf_op jit(solution)/shard_map/while/body/eval_jaxpr/cond/branch_1_fun/hgij,ihgd->jhd/dot_general | solution.py:193
  403.1 37.8 %conditional.4 = ((f32[256,512]{0,1:T(8,128)S(1)}, f32[256,512]{0,1:T(8,128)S(1)})) conditional(s32[]{:T(128)} %convert_element_type.67, (f32[256,512]{0,1:T(8,128)S(1)}, f32[256,512]{0,1:T(8,128)S(1)}) %tuple.141, (s32[]{:T(128)}, bf16[2048,4096]{0,1:T(8,128)(2,1)}, s32[]{:T(128)}, s32[512]{0:T(512)S(1)}, bf16[256,4,128]{2,0,1:T(8,128)(2,1)S(1)}, ...), branch_computations={%region_12.12_spmd, %region_13.13_spmd} | conditional | flops 4337303552 | bytes 106239080 | solution.py:201
  403.3 2.5 constant_dynamic-slice_fusion.1
  405.8 5.9 %constant_dynamic-slice_fusion = bf16[512,4096]{0,1:T(8,128)(2,1)} fusion(bf16[2048,4096]{0,1:T(8,128)(2,1)} %get-tuple-element.451, s32[]{:T(128)S(6)} %select_n.83), kind=kLoop, calls=%fused_computation.21 | loop fusion | bytes 8388612 | tf_op jit(solution)/shard_map/while/body/eval_jaxpr/cond/branch_1_fun/dynamic_slice | solution.py:168
  411.7 8.1 %fusion.18 = f32[4,512,8,256]{3,1,2,0:T(8,128)} fusion(bf16[512,4,8,128]{0,3,2,1:T(8,128)(2,1)S(1)} %bitcast.220, bf16[256,4,128]{2,0,1:T(8,128)(2,1)S(1)} %get-tuple-element.449), kind=kOutput, calls=%fused_computation.16 | convolution fusion | flops 1073741824 | bytes 21233664 | tf_op jit(solution)/shard_map/while/body/eval_jaxpr/cond/branch_1_fun/ihgd,jhd->hgij/dot_general | solution.py:178
  419.8 11.8 %fusion.15 = f32[4,128,256,1]{2,1,3,0:T(8,128)S(1)} fusion(bf16[512,4,8,128]{0,3,2,1:T(8,128)(2,1)} %bitcast.221, f32[4,512,8,256]{3,1,2,0:T(8,128)} %fusion.18, bf16[512,4,8,128]{0,3,2,1:T(8,128)(2,1)} %bitcast.222, f32[4,8,512]{2,1,0:T(8,128)S(1)} %dynamic-slice_bitcast_fusion, f32[4,8,512]{2,1,0:T(8,128)S(1)} %dynamic-slice_bitcast_fusion.1, ...), kind=kOutput, calls=%fused_computation.12 | convolution fusion | flops 2172649472 | bytes 26214400 | tf_op jit(solution)/shard_map/while/body/eval_jaxpr/cond/branch_1_fun/hgij,ihgd->jhd/dot_general | solution.py:190
  431.6 9.1 %fusion.12 = f32[4,128,256,1]{2,1,3,0:T(8,128)S(1)} fusion(bf16[512,4,8,128]{0,3,2,1:T(8,128)(2,1)} %bitcast.223, f32[4,512,8,256]{3,1,2,0:T(8,128)} %fusion.18, f32[4,8,512]{2,1,0:T(8,128)S(1)} %dynamic-slice_bitcast_fusion.1, pred[512,256]{1,0:T(8,128)(4,1)S(1)} %broadcast_compare_fusion), kind=kOutput, calls=%fused_computation.10 | convolution fusion | flops 1090519040 | bytes 21692416 | tf_op jit(solution)/shard_map/while/body/eval_jaxpr/cond/branch_1_fun/hgij,ihgd->jhd/dot_general | solution.py:193
  442.2 37.8 %conditional.4 = ((f32[256,512]{0,1:T(8,128)S(1)}, f32[256,512]{0,1:T(8,128)S(1)})) conditional(s32[]{:T(128)} %convert_element_type.67, (f32[256,512]{0,1:T(8,128)S(1)}, f32[256,512]{0,1:T(8,128)S(1)}) %tuple.141, (s32[]{:T(128)}, bf16[2048,4096]{0,1:T(8,128)(2,1)}, s32[]{:T(128)}, s32[512]{0:T(512)S(1)}, bf16[256,4,128]{2,0,1:T(8,128)(2,1)S(1)}, ...), branch_computations={%region_12.12_spmd, %region_13.13_spmd} | conditional | flops 4337303552 | bytes 106239080 | solution.py:201
  442.5 2.5 constant_dynamic-slice_fusion.1
  444.9 5.9 %constant_dynamic-slice_fusion = bf16[512,4096]{0,1:T(8,128)(2,1)} fusion(bf16[2048,4096]{0,1:T(8,128)(2,1)} %get-tuple-element.451, s32[]{:T(128)S(6)} %select_n.83), kind=kLoop, calls=%fused_computation.21 | loop fusion | bytes 8388612 | tf_op jit(solution)/shard_map/while/body/eval_jaxpr/cond/branch_1_fun/dynamic_slice | solution.py:168
  450.9 8.1 %fusion.18 = f32[4,512,8,256]{3,1,2,0:T(8,128)} fusion(bf16[512,4,8,128]{0,3,2,1:T(8,128)(2,1)S(1)} %bitcast.220, bf16[256,4,128]{2,0,1:T(8,128)(2,1)S(1)} %get-tuple-element.449), kind=kOutput, calls=%fused_computation.16 | convolution fusion | flops 1073741824 | bytes 21233664 | tf_op jit(solution)/shard_map/while/body/eval_jaxpr/cond/branch_1_fun/ihgd,jhd->hgij/dot_general | solution.py:178
  459.0 11.8 %fusion.15 = f32[4,128,256,1]{2,1,3,0:T(8,128)S(1)} fusion(bf16[512,4,8,128]{0,3,2,1:T(8,128)(2,1)} %bitcast.221, f32[4,512,8,256]{3,1,2,0:T(8,128)} %fusion.18, bf16[512,4,8,128]{0,3,2,1:T(8,128)(2,1)} %bitcast.222, f32[4,8,512]{2,1,0:T(8,128)S(1)} %dynamic-slice_bitcast_fusion, f32[4,8,512]{2,1,0:T(8,128)S(1)} %dynamic-slice_bitcast_fusion.1, ...), kind=kOutput, calls=%fused_computation.12 | convolution fusion | flops 2172649472 | bytes 26214400 | tf_op jit(solution)/shard_map/while/body/eval_jaxpr/cond/branch_1_fun/hgij,ihgd->jhd/dot_general | solution.py:190
  470.8 9.1 %fusion.12 = f32[4,128,256,1]{2,1,3,0:T(8,128)S(1)} fusion(bf16[512,4,8,128]{0,3,2,1:T(8,128)(2,1)} %bitcast.223, f32[4,512,8,256]{3,1,2,0:T(8,128)} %fusion.18, f32[4,8,512]{2,1,0:T(8,128)S(1)} %dynamic-slice_bitcast_fusion.1, pred[512,256]{1,0:T(8,128)(4,1)S(1)} %broadcast_compare_fusion), kind=kOutput, calls=%fused_computation.10 | convolution fusion | flops 1090519040 | bytes 21692416 | tf_op jit(solution)/shard_map/while/body/eval_jaxpr/cond/branch_1_fun/hgij,ihgd->jhd/dot_general | solution.py:193
  481.4 37.8 %conditional.4 = ((f32[256,512]{0,1:T(8,128)S(1)}, f32[256,512]{0,1:T(8,128)S(1)})) conditional(s32[]{:T(128)} %convert_element_type.67, (f32[256,512]{0,1:T(8,128)S(1)}, f32[256,512]{0,1:T(8,128)S(1)}) %tuple.141, (s32[]{:T(128)}, bf16[2048,4096]{0,1:T(8,128)(2,1)}, s32[]{:T(128)}, s32[512]{0:T(512)S(1)}, bf16[256,4,128]{2,0,1:T(8,128)(2,1)S(1)}, ...), branch_computations={%region_12.12_spmd, %region_13.13_spmd} | conditional | flops 4337303552 | bytes 106239080 | solution.py:201
  481.6 2.5 constant_dynamic-slice_fusion.1
  484.1 5.9 %constant_dynamic-slice_fusion = bf16[512,4096]{0,1:T(8,128)(2,1)} fusion(bf16[2048,4096]{0,1:T(8,128)(2,1)} %get-tuple-element.451, s32[]{:T(128)S(6)} %select_n.83), kind=kLoop, calls=%fused_computation.21 | loop fusion | bytes 8388612 | tf_op jit(solution)/shard_map/while/body/eval_jaxpr/cond/branch_1_fun/dynamic_slice | solution.py:168
  490.0 8.1 %fusion.18 = f32[4,512,8,256]{3,1,2,0:T(8,128)} fusion(bf16[512,4,8,128]{0,3,2,1:T(8,128)(2,1)S(1)} %bitcast.220, bf16[256,4,128]{2,0,1:T(8,128)(2,1)S(1)} %get-tuple-element.449), kind=kOutput, calls=%fused_computation.16 | convolution fusion | flops 1073741824 | bytes 21233664 | tf_op jit(solution)/shard_map/while/body/eval_jaxpr/cond/branch_1_fun/ihgd,jhd->hgij/dot_general | solution.py:178
  498.2 11.8 %fusion.15 = f32[4,128,256,1]{2,1,3,0:T(8,128)S(1)} fusion(bf16[512,4,8,128]{0,3,2,1:T(8,128)(2,1)} %bitcast.221, f32[4,512,8,256]{3,1,2,0:T(8,128)} %fusion.18, bf16[512,4,8,128]{0,3,2,1:T(8,128)(2,1)} %bitcast.222, f32[4,8,512]{2,1,0:T(8,128)S(1)} %dynamic-slice_bitcast_fusion, f32[4,8,512]{2,1,0:T(8,128)S(1)} %dynamic-slice_bitcast_fusion.1, ...), kind=kOutput, calls=%fused_computation.12 | convolution fusion | flops 2172649472 | bytes 26214400 | tf_op jit(solution)/shard_map/while/body/eval_jaxpr/cond/branch_1_fun/hgij,ihgd->jhd/dot_general | solution.py:190
  510.0 9.1 %fusion.12 = f32[4,128,256,1]{2,1,3,0:T(8,128)S(1)} fusion(bf16[512,4,8,128]{0,3,2,1:T(8,128)(2,1)} %bitcast.223, f32[4,512,8,256]{3,1,2,0:T(8,128)} %fusion.18, f32[4,8,512]{2,1,0:T(8,128)S(1)} %dynamic-slice_bitcast_fusion.1, pred[512,256]{1,0:T(8,128)(4,1)S(1)} %broadcast_compare_fusion), kind=kOutput, calls=%fused_computation.10 | convolution fusion | flops 1090519040 | bytes 21692416 | tf_op jit(solution)/shard_map/while/body/eval_jaxpr/cond/branch_1_fun/hgij,ihgd->jhd/dot_general | solution.py:193
  520.4 4.0 collective-permute-start.1
  524.4 1.8 broadcast_multiply_fusion
  526.2 1.8 copy.117
  (115 shorter events, 34.7 us)
Async XLA Ops:
  7.2 4.9 copy-start.3
  7.2 5.0 copy-start.4
  7.2 331.7 %all-gather.2.cloned.1.call-start = ((), (), s32[]{:S(2)}) async-start(), calls=%async_computation.1 | async-start | bytes 35651584 | tf_op jit(solution)/shard_map/all_gather | solution.py:23
  12.3 1.9 collective-permute-start
  14.4 4.4 copy-start.1
  18.8 144.1 %all-to-all-start = ((bf16[16,2,256,512]{3,2,1,0:T(8,128)(2,1)}), bf16[16,2,256,512]{3,2,1,0:T(8,128)(2,1)}, u32[]{:S(2)}, u32[]{:S(2)}) async-start(bf16[16,2,256,512]{3,2,1,0:T(8,128)(2,1)} %stack.14), calls=%async_computation | async-start | bytes 16777216 | tf_op jit(solution)/shard_map/all_to_all | solution.py:12
  338.9 23.6 %copy-start.2 = (bf16[256,4,128]{2,0,1:T(8,128)(2,1)S(1)}, bf16[256,4,128]{2,0,1:T(8,128)(2,1)}, u32[]{:S(2)}) copy-start(bf16[256,4,128]{2,0,1:T(8,128)(2,1)} %copy.97) | copy-start | bytes 786436
  366.6 5.9 %copy-start = (bf16[512,4096]{0,1:T(8,128)(2,1)}, bf16[512,4096]{0,1:T(8,128)(2,1)S(1)}, u32[]{:S(2)}) copy-start(bf16[512,4096]{0,1:T(8,128)(2,1)S(1)} %constant_dynamic-slice_fusion.1) | copy-start | bytes 12582916 | tf_op jit(solution)/shard_map/while/body/eval_jaxpr/cond
  405.8 5.9 %copy-start = (bf16[512,4096]{0,1:T(8,128)(2,1)}, bf16[512,4096]{0,1:T(8,128)(2,1)S(1)}, u32[]{:S(2)}) copy-start(bf16[512,4096]{0,1:T(8,128)(2,1)S(1)} %constant_dynamic-slice_fusion.1) | copy-start | bytes 12582916 | tf_op jit(solution)/shard_map/while/body/eval_jaxpr/cond
  444.9 5.9 %copy-start = (bf16[512,4096]{0,1:T(8,128)(2,1)}, bf16[512,4096]{0,1:T(8,128)(2,1)S(1)}, u32[]{:S(2)}) copy-start(bf16[512,4096]{0,1:T(8,128)(2,1)S(1)} %constant_dynamic-slice_fusion.1) | copy-start | bytes 12582916 | tf_op jit(solution)/shard_map/while/body/eval_jaxpr/cond
  484.1 5.9 %copy-start = (bf16[512,4096]{0,1:T(8,128)(2,1)}, bf16[512,4096]{0,1:T(8,128)(2,1)S(1)}, u32[]{:S(2)}) copy-start(bf16[512,4096]{0,1:T(8,128)(2,1)S(1)} %constant_dynamic-slice_fusion.1) | copy-start | bytes 12582916 | tf_op jit(solution)/shard_map/while/body/eval_jaxpr/cond
  520.4 7.6 %collective-permute-start.1 = (bf16[2,128,512]{2,1,0:T(8,128)(2,1)}, bf16[2,128,512]{2,1,0:T(8,128)(2,1)S(1)}, u32[]{:S(2)}, u32[]{:S(2)}) collective-permute-start(bf16[2,128,512]{2,1,0:T(8,128)(2,1)} %pad_maximum_fusion.2), channel_id=1, source_target_pairs={{0,1},{1,0},{2,3},{3,2},{4,5},{5,4},{6,7},{7,6},{8,9},{9,8},{10,11... | collective-permute-start | bytes 786440 | tf_op jit(solution)/shard_map/ppermute | solution.py:18
Sparse Core Ops, SparseCore 0:
  12.1 306.9 all-gather.1
